TPU v7x, 32 devices: a whole 2x2x4 slice. The times are simulated.
32 devices in a mesh: section: 4 (over x, core), shard: 8 (over z, y).
Axes of the slice: x: 2, y: 2, z: 4, core: 2. Of those that a mesh axis runs over, the one named last changes fastest.
Arguments:
- features: bfloat16 [2048, 6144], P('shard', 'section'), may hold values from -0.29882812 to 0.29882812
- proj_weight: bfloat16 [6144, 1024], P('section'), may hold values from -0.078125 to 0.078125
- captions: bfloat16 [32, 1024], P('shard'), may hold values from -6 to 6
- positives: int32 [2048], P('shard'), may hold values from 0 to 31
Outputs:
- region_grad: bfloat16 [2048, 6144], P('shard', 'section')
- caption_grad: float32 [32, 1024], P('shard')
All inputs are finite; a program needn't handle non-finite values.
Results may differ from a plain program's by a relative error of at most 0.0062.
Values may be sent and summed in bfloat16 or wider, within the bound.
A program may use at most 64 MiB of HBM per device.

v0:
```python
import jax
import jax.numpy as jnp
from jax import lax
from jax.sharding import PartitionSpec as P

logit_scale = 14.0
eps_norm = 1e-06


def term_maker(dlogits, region_rows):
    return logit_scale * lax.dot_general(
        dlogits, region_rows, (((0,), (0,)), ((), ())), preferred_element_type=jnp.float32
    )


def on_device(features, proj_weight, captions, positives):
    caption_float = captions.astype(jnp.float32)
    caption_scale = lax.rsqrt(
        jnp.sum(caption_float * caption_float, axis=1, keepdims=True) + eps_norm
    )
    caption_unit = caption_float * caption_scale
    caption_half = caption_unit.astype(jnp.bfloat16)
    caption_table = lax.all_gather(caption_half, "shard", axis=0, tiled=True)
    partial_value = jnp.dot(features, proj_weight, preferred_element_type=jnp.float32)
    projected = lax.psum(partial_value, "section")
    region_scale = lax.rsqrt(jnp.sum(projected * projected, axis=1, keepdims=True) + eps_norm)
    region_unit = projected * region_scale
    region_half = region_unit.astype(jnp.bfloat16)
    logits = logit_scale * lax.dot_general(
        region_half, caption_table, (((1,), (1,)), ((), ())), preferred_element_type=jnp.float32
    )
    expon = jnp.exp(logits)
    probs = expon / jnp.sum(expon, axis=1, keepdims=True)
    column_ids = lax.broadcasted_iota(jnp.int32, probs.shape, 1)
    onehot = (column_ids == positives[:, None]).astype(jnp.float32)
    dlogits = (probs - onehot).astype(jnp.bfloat16)
    dunit = logit_scale * jnp.dot(dlogits, caption_table, preferred_element_type=jnp.float32)
    dprojected = (
        region_scale * (dunit - region_unit * jnp.sum(region_unit * dunit, axis=1, keepdims=True))
    ).astype(jnp.bfloat16)
    dcaption = lax.psum_scatter(
        term_maker(dlogits, region_half), "shard", scatter_dimension=0, tiled=True
    )
    region_grad = lax.dot_general(
        dprojected, proj_weight, (((1,), (1,)), ((), ())), preferred_element_type=jnp.float32
    ).astype(jnp.bfloat16)
    caption_grad = caption_scale * (
        dcaption - caption_unit * jnp.sum(caption_unit * dcaption, axis=1, keepdims=True)
    )
    return (region_grad, caption_grad)


def solution(mesh):
    placed = (P("shard", "section"), P("section", None), P("shard", None), P("shard"))
    return jax.shard_map(
        on_device,
        mesh=mesh,
        in_specs=placed,
        out_specs=(P("shard", "section"), P("shard", None)),
        check_vma=False,
    )
```

profile of v0, /device:TPU:0, one launch (start us, length us, event | category | flops | bytes accessed | tf_op | source)
XLA Modules:
  0.0 135.7 jit_solution(17607319841420705687)
XLA Ops:
  7.2 0.0 copy-start
  7.2 0.0 copy-start.3
  7.2 0.0 copy-start.1
  7.2 0.0 copy-start.2
  7.2 0.0 all-reduce.4.cloned.1.call-start
  7.3 1.8 %copy-done = bf16[1536,1024]{1,0:T(8,128)(2,1)S(1)} copy-done((bf16[1536,1024]{1,0:T(8,128)(2,1)S(1)}, bf16[1536,1024]{1,0:T(8,128)(2,1)}, u32[]{:S(2)}) %copy-start) | copy-done | bytes 3145752
  9.1 3.1 %fusion.12 = f32[256,1024]{1,0:T(8,128)} fusion(bf16[256,1536]{1,0:T(8,128)(2,1)} %param.4, bf16[1536,1024]{1,0:T(8,128)(2,1)S(1)} %copy-done), kind=kOutput, calls=%fused_computation.26 | convolution fusion | flops 805306368 | bytes 4980736 | tf_op jit(solution)/shard_map/dot_general | solution.py:24
  12.2 0.0 all-reduce.4.cloned.1.call-update
  12.2 0.0 all-reduce.6.cloned.1.call-start
  12.3 0.0 copy-done.1
  12.3 0.1 fusion.9
  12.4 0.1 fusion.10
  12.5 32.3 %all-gather = bf16[8,4,1024]{2,1,0:T(4,128)(2,1)S(1)} all-gather(bf16[1,4,1024]{2,1,0:T(4,128)(2,1)S(1)} %fusion.10), channel_id=1, replica_groups=mesh['section'=4,'shard'=8] {'shard'}, dimensions={0}, use_global_device_ids=true | all-gather | bytes 73728 | tf_op jit(solution)/shard_map/all_gather | solution.py:23
  44.8 0.0 copy-done.3
  44.8 0.6 dynamic-slice
  46.1 5.2 %all-reduce.4.cloned.1.call-done = f32[256,1024]{1,0:T(8,128)} async-done(((f32[256,1024]{1,0:T(8,128)}), f32[256,1024]{1,0:T(8,128)}) %all-reduce.4.cloned.1.call-update) | async-done | bytes 1048592 | tf_op jit(solution)/shard_map/psum | solution.py:25
  51.2 1.4 %multiply_reduce_fusion.1 = f32[256]{0:T(256)S(1)} fusion(f32[256,1024]{1,0:T(8,128)} %all-reduce.4.cloned.1.call-done), kind=kLoop, calls=%fused_computation.7 | loop fusion | flops 524032 | bytes 1049600 | tf_op jit(solution)/shard_map/reduce_sum | solution.py:26
  52.6 1.6 %fusion.11 = (f32[256]{0:T(256)S(1)}, f32[256,32]{0,1:T(8,128)S(1)}) fusion(bf16[32,1024]{1,0:T(8,128)(2,1)S(1)} %reshape.21, f32[256,1024]{1,0:T(8,128)} %all-reduce.4.cloned.1.call-done, f32[256]{0:T(256)S(1)} %add_rsqrt_fusion), kind=kOutput, calls=%fused_computation.25 | convolution fusion | flops 17317632 | bytes 1148928 | tf_op jit(solution)/shard_map/dot_general | solution.py:29
  54.2 0.0 copy-done.2
  54.2 2.1 %convolution_multiply_fusion.1 = f32[32,1024]{1,0:T(8,128)} fusion(f32[256,32]{0,1:T(8,128)S(1)} %get-tuple-element.3, s32[256]{0:T(256)S(1)} %copy-done.2, f32[256]{0:T(256)S(1)} %get-tuple-element.2, f32[256,1024]{1,0:T(8,128)} %all-reduce.4.cloned.1.call-done, f32[256]{0:T(256)S(1)} %add_rsqrt_fusion), kind=kOutput, calls=%fused_computation.2 | convolution fusion | flops 17375232 | bytes 1215488 | tf_op jit(solution)/shard_map/dot_general | solution.py:11
  56.4 0.0 all-reduce.6.cloned.1.call-update
  56.4 1.6 %multiply_reduce_fusion = (f32[256]{0:T(256)S(1)}, f32[256,1024]{1,0:T(8,128)S(1)}) fusion(f32[256,1024]{1,0:T(8,128)} %all-reduce.4.cloned.1.call-done, f32[256]{0:T(256)S(1)} %add_rsqrt_fusion, bf16[32,1024]{1,0:T(8,128)(2,1)S(1)} %reshape.21, f32[256,32]{0,1:T(8,128)S(1)} %get-tuple-element.3, s32[256]{0:T(256)S(1)} %copy-done.2, f32[256]{0:T(256)S(1)} %get-tuple-element.2), kind=kOutput, calls=%fused_computation.6 | convolution fusion | flops 17866496 | bytes 2199552 | tf_op jit(solution)/shard_map/dot_general | solution.py:37
  58.0 3.3 %convolution_convert_fusion = bf16[256,1536]{1,0:T(8,128)(2,1)} fusion(bf16[1536,1024]{1,0:T(8,128)(2,1)S(1)} %copy-done, f32[256,1024]{1,0:T(8,128)S(1)} %get-tuple-element.5, f32[256,1024]{1,0:T(8,128)} %all-reduce.4.cloned.1.call-done, f32[256]{0:T(256)S(1)} %get-tuple-element.4, f32[256]{0:T(256)S(1)} %add_rsqrt_fusion), kind=kOutput, calls=%fused_computation | convolution fusion | flops 807010304 | bytes 6031360 | tf_op jit(solution)/shard_map/dot_general | solution.py:44
  61.3 65.1 %all-reduce.6.cloned.1.call-done = f32[32,1024]{1,0:T(8,128)} async-done(((f32[32,1024]{1,0:T(8,128)}), f32[32,1024]{1,0:T(8,128)}) %all-reduce.6.cloned.1.call-update) | async-done | bytes 131088
  126.4 0.9 fusion.6
  127.4 1.4 %fusion.8 = f32[4,1024]{1,0:T(4,128)} fusion(bf16[4,1024]{1,0:T(4,128)(2,1)S(1)} %copy-done.1, f32[32,1024]{1,0:T(8,128)} %all-reduce.6.cloned.1.call-done, u32[]{:T(128)S(6)} %multiply.1, f32[4]{0:T(128)S(1)} %fusion.6, f32[4]{0:T(128)S(1)} %add_rsqrt_fusion.1), kind=kLoop, calls=%fused_computation.20 | loop fusion | flops 20480 | bytes 40996 | tf_op jit(solution)/shard_map/mul | solution.py:47
  (3 shorter events, 0.0 us)
Async XLA Ops:
  7.2 1.9 %copy-start = (bf16[1536,1024]{1,0:T(8,128)(2,1)S(1)}, bf16[1536,1024]{1,0:T(8,128)(2,1)}, u32[]{:S(2)}) copy-start(bf16[1536,1024]{1,0:T(8,128)(2,1)} %param.5) | copy-start | bytes 9437188
  7.2 37.6 %copy-start.3 = (u32[32]{0:T(128)S(1)}, u32[32]{0:T(128)}, u32[]{:S(2)}) copy-start(u32[32]{0:T(128)} %constant.12) | copy-start | bytes 388
  7.2 5.1 %copy-start.1 = (bf16[4,1024]{1,0:T(4,128)(2,1)S(1)}, bf16[4,1024]{1,0:T(4,128)(2,1)}, u32[]{:S(2)}) copy-start(bf16[4,1024]{1,0:T(4,128)(2,1)} %param.6) | copy-start | bytes 24580
  7.2 47.0 %copy-start.2 = (s32[256]{0:T(256)S(1)}, s32[256]{0:T(256)}, u32[]{:S(2)}) copy-start(s32[256]{0:T(256)} %param.7) | copy-start | bytes 3076
  7.2 44.0 %all-reduce.4.cloned.1.call-start = ((), (), s32[]{:S(2)}) async-start(), calls=%async_computation | async-start | bytes 2097152 | tf_op jit(solution)/shard_map/psum | solution.py:25
  12.2 114.2 %all-reduce.6.cloned.1.call-start = ((), (), s32[]{:S(2)}) async-start(), calls=%async_computation.1 | async-start | bytes 262144
Sparse Core Ops, SparseCore 0:
  12.4 38.8 all-reduce.3
  56.5 69.8 all-reduce.5
where the time goes:
time: 136 us
  waiting for transfers between devices  70.3 us (52%)
  blocking collectives  32.3 us (24%)
  between operations  14.8 us (11%)
  matrix products  11.8 us (9%)
  other arithmetic  3.97 us (3%)
  local copies, waits for them, and re-layouts  2.44 us (2%)
    unnamed x3, waiting for transfers between devices  65.2 us
    all_gather x1, blocking collectives, on_device(): caption_table = lax.all_gather(caption_half, 'shard', axis=0, tiled=True)  32.3 us
    psum x1, waiting for transfers between devices, on_device(): projected = lax.psum(partial_value, 'section')  5.17 us
    dot_general x1, matrix products, on_device(): lax.dot_general(dprojected, proj_weight, (((1,), (1,)), ((), ())), prefer...  3.27 us
    dot_general x1, matrix products, on_device(): jnp.dot(features, proj_weight, preferred_element_type=jnp.float32)  3.15 us
  transfers between devices with their start and end apart: 2, of which 2 were waited for; matrix products, arithmetic and copies ran while one was open for 4% of the time, Pallas kernels for 0%

commit v1 on v0

v1 whole, which is shorter than its diff:
```python
import functools

import jax
import jax.numpy as jnp
from jax import lax
from jax.experimental import pallas as pl
from jax.experimental.pallas import tpu as pltpu
from jax.sharding import PartitionSpec as P

logit_scale = 14.0
eps_norm = 1e-06
MESH = pl.DeviceIdType.MESH
F32 = jnp.float32
BF16 = jnp.bfloat16
SLOT = 16
CHUNKS = 4
PIECES = 3


def each(low, high, body):
    if high - low <= 8:
        for k in range(low, high):
            body(k)
    else:
        lax.fori_loop(low, high, lambda k, c: (body(k), c)[1], 0)


def kernel(
    sections, shards, f_hbm, w_hbm, cap_ref, pos_ref, rg_hbm, cg_ref,
    fv, wv, own, psnd, prcv, xr, dp, og, cs, tab, dacc, dpt, dsnd, drc,
    f_sem, w_sem, og_sem, ps_sem, pr_sem, xs_sem, xr_sem, ds_sem, dr_sem,
    cs_sem, cr_sem, as_sem, ar_sem, gs_sem, gr_sem,
):
    chips = sections // 2
    n_chunks, _, rows, depth = fv.shape
    width = wv.shape[1]
    half_rows = n_chunks * rows
    caps = cap_ref.shape[0]
    packs = SLOT // caps
    lanes = width // packs
    sec = lax.axis_index("section")
    t = lax.axis_index("shard")
    core = lax.rem(sec, 2)
    chip = sec // 2
    mate = chip * 2 + (1 - core)

    def chip_peer(k):
        return lax.rem(chip + k, chips)

    def shard_peer(k):
        return lax.rem(t + k, shards)

    def place(c, s):
        return {"section": c, "shard": s}

    def row_at(i, which):
        owner = core if which == 1 else 1 - core
        return pl.multiple_of(owner * half_rows + i * rows, rows)

    step = depth // PIECES

    def f_copy(i, which):
        return pltpu.make_async_copy(
            f_hbm.at[pl.ds(row_at(i, which), rows), :], fv.at[i, which], f_sem.at[i, which]
        )

    def w_copy(p):
        band = pl.ds(p * step, step)
        return pltpu.make_async_copy(w_hbm.at[band, :], wv.at[band, :], w_sem.at[p])

    def og_copy(i, which):
        return pltpu.make_async_copy(
            og.at[i, which], rg_hbm.at[pl.ds(row_at(i, which), rows), :], og_sem.at[i, which]
        )

    for which in range(2):
        f_copy(0, which).start()
    for p in range(PIECES):
        w_copy(p).start()
    for i in range(1, n_chunks):
        for which in range(2):
            f_copy(i, which).start()

    barrier = pltpu.get_barrier_semaphore()

    def greet(c, s):
        pl.semaphore_signal(barrier, inc=1, device_id=place(c, s), device_id_type=MESH)

    greet(mate, t)
    each(1, chips, lambda k: greet(chip_peer(k) * 2 + core, t))
    each(1, shards, lambda k: greet(sec, shard_peer(k)))

    cap_float = cap_ref[...].astype(F32)
    cap_scale = lax.rsqrt(jnp.sum(cap_float * cap_float, axis=1, keepdims=True) + eps_norm)
    cap_unit = cap_float * cap_scale
    packed = jnp.concatenate(
        [cap_unit[:, q * lanes : (q + 1) * lanes] for q in range(packs)], axis=0
    )
    cs[t] = packed.astype(BF16)

    pl.semaphore_wait(barrier, 1 + (chips - 1) + (shards - 1))

    def cap_copy(k, source):
        return pltpu.make_async_remote_copy(
            src_ref=cs.at[source], dst_ref=cs.at[source],
            send_sem=cs_sem.at[k], recv_sem=cr_sem.at[source],
            device_id=place(sec, shard_peer(k)), device_id_type=MESH,
        )

    each(1, shards, lambda k: cap_copy(k, t).start())

    def mate_copy(i):
        return pltpu.make_async_remote_copy(
            src_ref=psnd.at[i], dst_ref=prcv.at[i],
            send_sem=ps_sem.at[i], recv_sem=pr_sem.at[i],
            device_id=place(mate, t), device_id_type=MESH,
        )

    def chip_copy(k, i, source):
        return pltpu.make_async_remote_copy(
            src_ref=xr.at[source, i], dst_ref=xr.at[source, i],
            send_sem=xs_sem.at[k, i], recv_sem=xr_sem.at[source, i],
            device_id=place(chip_peer(k) * 2 + core, t), device_id_type=MESH,
        )

    def dp_copy(i):
        return pltpu.make_async_remote_copy(
            src_ref=dp.at[i, 1], dst_ref=dp.at[i, 0],
            send_sem=ds_sem.at[i], recv_sem=dr_sem.at[i],
            device_id=place(mate, t), device_id_type=MESH,
        )

    def chip_sum(i):
        mate_copy(i).wait_recv()
        xr[chip, i] = (own[i] + prcv[i].astype(F32)).astype(BF16)
        each(1, chips, lambda k: chip_copy(k, i, chip).start())

    for i in range(n_chunks):
        for which in range(2):
            f_copy(i, which).wait()
        if i == 0:
            part = None
            for p in range(PIECES):
                w_copy(p).wait()
                band = slice(p * step, (p + 1) * step)
                term = jnp.dot(
                    fv[i, :, :, band].reshape(2 * rows, step), wv[band, :],
                    preferred_element_type=F32,
                )
                part = term if part is None else part + term
        else:
            part = jnp.dot(
                fv[i].reshape(2 * rows, depth), wv[...], preferred_element_type=F32
            )
        psnd[i] = part[:rows].astype(BF16)
        mate_copy(i).start()
        own[i] = part[rows:]
        if i >= 1:
            chip_sum(i - 1)
    chip_sum(n_chunks - 1)

    each(1, shards, lambda k: cap_copy(k, shard_peer(k)).wait_recv())
    per = min(8, shards)
    group = per * SLOT
    ra = lax.broadcasted_iota(jnp.int32, (group, group), 0)
    rb = lax.broadcasted_iota(jnp.int32, (group, group), 1)
    same = jnp.logical_and(ra // SLOT == rb // SLOT, ra % caps == rb % caps)
    picks = [
        jnp.logical_and(same, (rb % SLOT) // caps == q).astype(F32).astype(BF16)
        for q in range(packs)
    ]
    for g in range(shards // per):
        block = cs[g * per : (g + 1) * per].reshape(group, lanes)
        for q in range(packs):
            tab[g * group : (g + 1) * group, q * lanes : (q + 1) * lanes] = jnp.dot(
                picks[q], block, preferred_element_type=F32
            ).astype(BF16)

    positives = pos_ref[...]
    positives = jnp.where(core == 0, positives[:, :half_rows], positives[:, half_rows:])
    total = shards * SLOT
    ids = lax.broadcasted_iota(jnp.int32, (total, rows), 0)
    ids = caps * (ids // SLOT) + ids % caps
    piece = (lax.broadcasted_iota(jnp.int32, (total, lanes), 0) % SLOT) // caps

    def score(i):
        each(1, chips, lambda k: chip_copy(k, i, chip_peer(k)).wait_recv())
        projected = xr[0, i].astype(F32)
        for c in range(1, chips):
            projected = projected + xr[c, i].astype(F32)
        scale = lax.rsqrt(jnp.sum(projected * projected, axis=1, keepdims=True) + eps_norm)
        unit = projected * scale
        half = unit.astype(BF16)
        logits = logit_scale * lax.dot_general(
            tab[...], half, (((1,), (1,)), ((), ())), preferred_element_type=F32
        )
        expon = jnp.exp(logits)
        probs = expon * (packs / jnp.sum(expon, axis=0, keepdims=True))
        onehot = (ids == positives[:, i * rows : (i + 1) * rows]).astype(F32)
        dlogits = (probs - onehot).astype(BF16)
        dunit = (logit_scale / packs) * lax.dot_general(
            dlogits, tab[...], (((0,), (0,)), ((), ())), preferred_element_type=F32
        )
        dproj = scale * (dunit - unit * jnp.sum(unit * dunit, axis=1, keepdims=True))
        dp[i, 1] = dproj.astype(BF16)
        dp_copy(i).start()
        term = jnp.zeros((total, lanes), F32)
        for q in range(packs):
            value = jnp.dot(
                dlogits, half[:, q * lanes : (q + 1) * lanes], preferred_element_type=F32
            )
            term = jnp.where(piece == q, value, term)
        dacc[...] = term if i == 0 else dacc[...] + term

    def grad(i):
        dp_copy(i).wait_recv()
        value = lax.dot_general(
            dp[i].reshape(2 * rows, width), wv[...], (((1,), (1,)), ((), ())),
            preferred_element_type=F32,
        ).astype(BF16)
        og[i] = value.reshape(2, rows, depth)
        for which in range(2):
            og_copy(i, which).start()

    sum_copy = pltpu.make_async_remote_copy(
        src_ref=dacc, dst_ref=dpt, send_sem=as_sem, recv_sem=ar_sem,
        device_id=place(mate, t), device_id_type=MESH,
    )

    def give_copy(k, there, here):
        return pltpu.make_async_remote_copy(
            src_ref=dsnd.at[there], dst_ref=drc.at[here],
            send_sem=gs_sem.at[k], recv_sem=gr_sem.at[here],
            device_id=place(sec, shard_peer(k)), device_id_type=MESH,
        )

    for i in range(n_chunks):
        score(i)
        if i == n_chunks - 1:
            sum_copy.start()
        if i >= 1:
            grad(i - 1)
    sum_copy.wait_recv()
    dsnd[...] = (dacc[...] + dpt[...]).astype(BF16).reshape(shards, SLOT, lanes)
    each(1, shards, lambda k: give_copy(k, shard_peer(k), t).start())
    drc[t] = dsnd[t]
    grad(n_chunks - 1)
    each(1, shards, lambda k: give_copy(k, shard_peer(k), shard_peer(k)).wait_recv())
    dcap = logit_scale * jnp.sum(drc[...].astype(F32), axis=0)
    dcap = jnp.concatenate(
        [dcap[q * caps : (q + 1) * caps, :] for q in range(packs)], axis=1
    )
    cg_ref[...] = cap_scale * (
        dcap - cap_unit * jnp.sum(cap_unit * dcap, axis=1, keepdims=True)
    )

    for i in range(n_chunks):
        for which in range(2):
            og_copy(i, which).wait()
        mate_copy(i).wait_send()
        dp_copy(i).wait_send()
        each(1, chips, lambda k: chip_copy(k, i, chip).wait_send())
    sum_copy.wait_send()
    each(1, shards, lambda k: cap_copy(k, t).wait_send())
    each(1, shards, lambda k: give_copy(k, shard_peer(k), t).wait_send())


def solution(mesh):
    sections, shards = mesh.shape["section"], mesh.shape["shard"]
    chips = sections // 2

    def on_device(features, proj_weight, captions, positives):
        n_rows, depth = features.shape
        width = proj_weight.shape[1]
        caps = captions.shape[0]
        lanes = width * caps // SLOT
        n = CHUNKS
        rows = n_rows // 2 // n
        dma = pltpu.SemaphoreType.DMA
        any_space = pl.BlockSpec(memory_space=pl.ANY)
        vmem = pl.BlockSpec(memory_space=pltpu.VMEM)
        flops = 4 * n_rows * depth * width
        return pl.pallas_call(
            functools.partial(kernel, sections, shards),
            out_shape=(
                jax.ShapeDtypeStruct((n_rows, depth), BF16),
                jax.ShapeDtypeStruct((caps, width), F32),
            ),
            in_specs=[any_space, any_space, vmem, vmem],
            out_specs=(any_space, vmem),
            scratch_shapes=[
                pltpu.VMEM((n, 2, rows, depth), BF16),
                pltpu.VMEM((depth, width), BF16),
                pltpu.VMEM((n, rows, width), F32),
                pltpu.VMEM((n, rows, width), BF16),
                pltpu.VMEM((n, rows, width), BF16),
                pltpu.VMEM((chips, n, rows, width), BF16),
                pltpu.VMEM((n, 2, rows, width), BF16),
                pltpu.VMEM((n, 2, rows, depth), BF16),
                pltpu.VMEM((shards, SLOT, lanes), BF16),
                pltpu.VMEM((shards * SLOT, width), BF16),
                pltpu.VMEM((shards * SLOT, lanes), F32),
                pltpu.VMEM((shards * SLOT, lanes), F32),
                pltpu.VMEM((shards, SLOT, lanes), BF16),
                pltpu.VMEM((shards, SLOT, lanes), BF16),
                dma((n, 2)), dma((PIECES,)), dma((n, 2)),
                dma((n,)), dma((n,)),
                dma((chips, n)), dma((chips, n)),
                dma((n,)), dma((n,)),
                dma((shards,)), dma((shards,)),
                dma, dma,
                dma((shards,)), dma((shards,)),
            ],
            cost_estimate=pl.CostEstimate(
                flops=flops,
                bytes_accessed=2 * (2 * n_rows * depth + depth * width),
                transcendentals=0,
            ),
            compiler_params=pltpu.CompilerParams(
                collective_id=0, has_side_effects=True, vmem_limit_bytes=56 * 1024 * 1024
            ),
        )(features, proj_weight, captions, positives.reshape(1, n_rows))

    return jax.shard_map(
        on_device,
        mesh=mesh,
        in_specs=(P("shard", "section"), P("section", None), P("shard", None), P("shard")),
        out_specs=(P("shard", "section"), P("shard", None)),
        check_vma=False,
    )
```

time: 136 us -> 28.6 us (0.21)
  waiting for transfers between devices: 70.3 us -> 0 us
  blocking collectives: 32.3 us -> 0 us
  Pallas kernels: 0 us -> 24.3 us
  between operations: 14.8 us -> 0.64 us
  matrix products: 11.8 us -> 0 us
  other arithmetic: 3.97 us -> 0 us
    unnamed x3 -> x0, waiting for transfers between devices: 65.2 us -> none
    all_gather x1 -> x0, blocking collectives: 32.3 us -> none  [on_device(): caption_table = lax.all_gather(caption_half, 'shard', axis=0, tiled=True)]
    pallas_call x0 -> x1, Pallas kernels: none -> 24.3 us  [on_device(): pl.pallas_call(functools.partial(kernel, sections, shards), out_shape=(ja...]
    dot_general x5 -> x0, matrix products: 11.8 us -> none  [the longest x1 3.27 us: on_device(): lax.dot_general(dprojected, proj_weight, (((1,), (1,)), ((), ())), prefer...]
    psum x1 -> x0, waiting for transfers between devices: 5.17 us -> none  [on_device(): projected = lax.psum(partial_value, 'section')]
    reduce_sum x3 -> x0, other arithmetic: 2.44 us -> none  [the longest x1 1.37 us: on_device(): jnp.sum(projected * projected, axis=1, keepdims=True) + eps_norm]
    mul x1 -> x0, other arithmetic: 1.44 us -> none  [on_device(): caption_scale * (dcaption - caption_unit * jnp.sum(caption_unit * dcaptio...]
    unnamed x10 -> x2, local copies, waits for them, and re-layouts: 2.44 us -> 3.39 us
  transfers between devices with their start and end apart: 2 -> 0, of which waited for: 2 -> 0; matrix products, arithmetic and copies ran while one was open for 4% -> 0% of each run, Pallas kernels for 0% -> 0%
where the time goes in v1:
time: 28.6 us; the launch traced here: 28.3 us
  Pallas kernels  24.3 us (85%)
  local copies, waits for them, and re-layouts  3.39 us (12%)
  between operations  0.64 us (2%)
    pallas_call x1, Pallas kernels, on_device(): pl.pallas_call(functools.partial(kernel, sections, shards), out_shape=(ja...  24.3 us
    unnamed x2, local copies, waits for them, and re-layouts  3.39 us

profile of v1, /device:TPU:0, one launch (start us, length us, event | category | flops | bytes accessed | tf_op | source)
XLA Modules:
  0.0 28.3 jit_solution(17148921588879548345)
XLA Ops:
  0.6 24.3 %shard_map.59 = (bf16[256,1536]{1,0:T(8,128)(2,1)}, f32[4,1024]{1,0:T(4,128)}) custom-call(bf16[256,1536]{1,0:T(8,128)(2,1)} %f_hbm.1, bf16[1536,1024]{1,0:T(8,128)(2,1)} %w_hbm.1, bf16[4,1024]{1,0:T(4,128)(2,1)} %cap_ref.1, s32[1,256]{1,0:T(1,128)} %bitcast.1), custom_call_target="tpu_custom_call" | custom-call | flops 1610612736 | bytes 4718592 | tf_op jit(solution)/shard_map/pallas_call | solution.py:283
  24.9 2.1 %copy.8 = bf16[256,1536]{1,0:T(8,128)(2,1)} copy(bf16[256,1536]{1,0:T(8,128)(2,1)} %get-tuple-element.4) | data formatting | bytes 1572864
  27.0 1.3 %copy.9 = f32[4,1024]{1,0:T(4,128)} copy(f32[4,1024]{1,0:T(4,128)} %get-tuple-element.5) | data formatting | bytes 32768

commit v2 on v1

--- a/solution.py
+++ b/solution.py
@@ -13,7 +13,8 @@
 F32 = jnp.float32
 BF16 = jnp.bfloat16
 SLOT = 16
-CHUNKS = 4
+CHUNKS = 2
+COPIES = 8
 PIECES = 3
 
 
@@ -265,6 +266,18 @@
     each(1, shards, lambda k: give_copy(k, shard_peer(k), t).wait_send())
 
 
+def write_out(rg_in, cg_in, rg_out, cg_out, sem):
+    rows = rg_in.shape[0] // COPIES
+    copies = [pltpu.make_async_copy(cg_in, cg_out, sem.at[COPIES])]
+    for i in range(COPIES):
+        band = pl.ds(i * rows, rows)
+        copies.append(pltpu.make_async_copy(rg_in.at[band, :], rg_out.at[band, :], sem.at[i]))
+    for copy in copies:
+        copy.start()
+    for copy in copies:
+        copy.wait()
+
+
 def solution(mesh):
     sections, shards = mesh.shape["section"], mesh.shape["shard"]
     chips = sections // 2
@@ -280,12 +293,13 @@
         any_space = pl.BlockSpec(memory_space=pl.ANY)
         vmem = pl.BlockSpec(memory_space=pltpu.VMEM)
         flops = 4 * n_rows * depth * width
-        return pl.pallas_call(
+        shapes = (
+            jax.ShapeDtypeStruct((n_rows, depth), BF16),
+            jax.ShapeDtypeStruct((caps, width), F32),
+        )
+        grads = pl.pallas_call(
             functools.partial(kernel, sections, shards),
-            out_shape=(
-                jax.ShapeDtypeStruct((n_rows, depth), BF16),
-                jax.ShapeDtypeStruct((caps, width), F32),
-            ),
+            out_shape=shapes,
             in_specs=[any_space, any_space, vmem, vmem],
             out_specs=(any_space, vmem),
             scratch_shapes=[
@@ -320,6 +334,16 @@
                 collective_id=0, has_side_effects=True, vmem_limit_bytes=56 * 1024 * 1024
             ),
         )(features, proj_weight, captions, positives.reshape(1, n_rows))
+        return pl.pallas_call(
+            write_out,
+            out_shape=shapes,
+            in_specs=[any_space, any_space],
+            out_specs=(any_space, any_space),
+            scratch_shapes=[dma((COPIES + 1,))],
+            cost_estimate=pl.CostEstimate(
+                flops=0, bytes_accessed=4 * n_rows * depth, transcendentals=0
+            ),
+        )(*grads)
 
     return jax.shard_map(
         on_device,

time: 28.6 us -> 49.7 us (1.74)
  Pallas kernels: 24.3 us -> 48.8 us
  local copies, waits for them, and re-layouts: 3.39 us -> 0 us
    pallas_call x1 -> x2, Pallas kernels: 24.3 us -> 48.8 us  [the longest x1 25.5 us: on_device(): pl.pallas_call(write_out, out_shape=shapes, in_specs=[any_space, any_spac...]
    unnamed x2 -> x0, local copies, waits for them, and re-layouts: 3.39 us -> none
where the time goes in v2:
time: 49.7 us; the launch traced here: 49.5 us
  Pallas kernels  48.8 us (98%)
  between operations  0.64 us (1%)
    pallas_call x1, Pallas kernels, on_device(): pl.pallas_call(write_out, out_shape=shapes, in_specs=[any_space, any_spac...  25.5 us
    pallas_call x1, Pallas kernels, on_device(): pl.pallas_call(functools.partial(kernel, sections, shards), out_shape=sha...  23.3 us

profile of v2, /device:TPU:0, one launch (start us, length us, event | category | flops | bytes accessed | tf_op | source)
XLA Modules:
  0.0 49.5 jit_solution(9448775431916612586)
XLA Ops:
  0.6 23.3 %shard_map.59 = (bf16[256,1536]{1,0:T(8,128)(2,1)}, f32[4,1024]{1,0:T(4,128)}) custom-call(bf16[256,1536]{1,0:T(8,128)(2,1)} %f_hbm.1, bf16[1536,1024]{1,0:T(8,128)(2,1)} %w_hbm.1, bf16[4,1024]{1,0:T(4,128)(2,1)} %cap_ref.1, s32[1,256]{1,0:T(1,128)} %bitcast.1), custom_call_target="tpu_custom_call" | custom-call | flops 1610612736 | bytes 4718592 | tf_op jit(solution)/shard_map/pallas_call | solution.py:300
  23.9 25.5 %shard_map.60 = (bf16[256,1536]{1,0:T(8,128)(2,1)}, f32[4,1024]{1,0:T(4,128)}) custom-call(bf16[256,1536]{1,0:T(8,128)(2,1)} %get-tuple-element.4.rg_in, f32[4,1024]{1,0:T(4,128)} %get-tuple-element.5.cg_in), custom_call_target="tpu_custom_call" | custom-call | bytes 1572864 | tf_op jit(solution)/shard_map/pallas_call | solution.py:337

commit v3 on v2

v3 whole, which is shorter than its diff:
```python
import functools

import jax
import jax.numpy as jnp
from jax import lax
from jax.experimental import pallas as pl
from jax.experimental.pallas import tpu as pltpu
from jax.sharding import PartitionSpec as P

logit_scale = 14.0
eps_norm = 1e-06
MESH = pl.DeviceIdType.MESH
F32 = jnp.float32
BF16 = jnp.bfloat16
SLOT = 16
CHUNKS = 2
COPIES = 4
PIECES = 3


def each(low, high, body):
    if high - low <= 8:
        for k in range(low, high):
            body(k)
    else:
        lax.fori_loop(low, high, lambda k, c: (body(k), c)[1], 0)


def kernel(
    sections, shards, f_hbm, w_hbm, cap_ref, pos_ref, rg_hbm, cg_ref,
    fv, wv, own, psnd, prcv, xs, xr, dp, og, cs, tab, dacc, dpt, dsnd, drc, fin,
    f_sem, w_sem, og_sem, ps_sem, pr_sem, xs_sem, xr_sem, ms_sem, mr_sem, ds_sem, dr_sem,
    cs_sem, cr_sem, as_sem, ar_sem, gs_sem, gr_sem, es_sem, er_sem,
):
    chips = sections // 2
    n_chunks, _, _, rows, width = dp.shape
    depth = wv.shape[0]
    half = chips * rows
    both = 2 * half
    caps = cap_ref.shape[0]
    packs = SLOT // caps
    lanes = width // packs
    sec = lax.axis_index("section")
    t = lax.axis_index("shard")
    core = lax.rem(sec, 2)
    chip = sec // 2
    mate = chip * 2 + (1 - core)

    def chip_peer(k):
        return lax.rem(chip + k, chips)

    def shard_peer(k):
        return lax.rem(t + k, shards)

    def place(c, s):
        return {"section": c, "shard": s}

    def to_mate(src, dst, send, recv):
        return pltpu.make_async_remote_copy(
            src_ref=src, dst_ref=dst, send_sem=send, recv_sem=recv,
            device_id=place(mate, t), device_id_type=MESH,
        )

    def to_chip(k, src, dst, send, recv):
        return pltpu.make_async_remote_copy(
            src_ref=src, dst_ref=dst, send_sem=send, recv_sem=recv,
            device_id=place(chip_peer(k) * 2 + core, t), device_id_type=MESH,
        )

    def to_shard(k, src, dst, send, recv):
        return pltpu.make_async_remote_copy(
            src_ref=src, dst_ref=dst, send_sem=send, recv_sem=recv,
            device_id=place(sec, shard_peer(k)), device_id_type=MESH,
        )

    step = depth // PIECES

    def f_copy(i, which):
        owner = core if which == 1 else 1 - core
        start = pl.multiple_of(i * both + owner * half, half)
        return pltpu.make_async_copy(
            f_hbm.at[pl.ds(start, half), :], fv.at[i, which], f_sem.at[i, which]
        )

    def w_copy(p):
        band = pl.ds(p * step, step)
        return pltpu.make_async_copy(w_hbm.at[band, :], wv.at[band, :], w_sem.at[p])

    def og_copy(i):
        return pltpu.make_async_copy(
            og.at[i], rg_hbm.at[pl.ds(i * both, both), :], og_sem.at[i]
        )

    for which in range(2):
        f_copy(0, which).start()
    for p in range(PIECES):
        w_copy(p).start()
    for i in range(1, n_chunks):
        for which in range(2):
            f_copy(i, which).start()

    barrier = pltpu.get_barrier_semaphore()

    def greet(c, s):
        pl.semaphore_signal(barrier, inc=1, device_id=place(c, s), device_id_type=MESH)

    greet(mate, t)
    each(1, chips, lambda k: greet(chip_peer(k) * 2 + core, t))
    each(1, shards, lambda k: greet(sec, shard_peer(k)))

    cap_float = cap_ref[...].astype(F32)
    cap_scale = lax.rsqrt(jnp.sum(cap_float * cap_float, axis=1, keepdims=True) + eps_norm)
    cap_unit = cap_float * cap_scale
    packed = jnp.concatenate(
        [cap_unit[:, q * lanes : (q + 1) * lanes] for q in range(packs)], axis=0
    )
    cs[t] = packed.astype(BF16)

    def cap_copy(k, source):
        return to_shard(k, cs.at[source], cs.at[source], cs_sem.at[k], cr_sem.at[source])

    def mate_copy(i):
        return to_mate(psnd.at[i], prcv.at[i], ps_sem.at[i], pr_sem.at[i])

    def part_copy(k, i, there, here):
        return to_chip(k, xs.at[i, there], xr.at[here, i], xs_sem.at[k, i], xr_sem.at[here, i])

    def chip_sum(i):
        mate_copy(i).wait_recv()
        value = own[i] + prcv[i].astype(F32)
        own[i] = value
        xs[i] = value.astype(BF16).reshape(chips, rows, width)
        each(1, chips, lambda k: part_copy(k, i, chip_peer(k), chip).start())

    for i in range(n_chunks):
        for which in range(2):
            f_copy(i, which).wait()
        if i == 0:
            part = None
            for p in range(PIECES):
                w_copy(p).wait()
                band = slice(p * step, (p + 1) * step)
                term = jnp.dot(
                    fv[i, :, :, band].reshape(both, step), wv[band, :],
                    preferred_element_type=F32,
                )
                part = term if part is None else part + term
        else:
            part = jnp.dot(fv[i].reshape(both, depth), wv[...], preferred_element_type=F32)
        psnd[i] = part[:half].astype(BF16)
        own[i] = part[half:]
        if i == 0:
            pl.semaphore_wait(barrier, 1 + (chips - 1) + (shards - 1))
        mate_copy(i).start()
        if i == 0:
            each(1, shards, lambda k: cap_copy(k, t).start())
        if i >= 1:
            chip_sum(i - 1)
    chip_sum(n_chunks - 1)

    each(1, shards, lambda k: cap_copy(k, shard_peer(k)).wait_recv())
    per = min(8, shards)
    group = per * SLOT
    ra = lax.broadcasted_iota(jnp.int32, (group, group), 0)
    rb = lax.broadcasted_iota(jnp.int32, (group, group), 1)
    same = jnp.logical_and(ra // SLOT == rb // SLOT, ra % caps == rb % caps)
    picks = [
        jnp.logical_and(same, (rb % SLOT) // caps == q).astype(F32).astype(BF16)
        for q in range(packs)
    ]
    for g in range(shards // per):
        block = cs[g * per : (g + 1) * per].reshape(group, lanes)
        for q in range(packs):
            tab[g * group : (g + 1) * group, q * lanes : (q + 1) * lanes] = jnp.dot(
                picks[q], block, preferred_element_type=F32
            ).astype(BF16)

    positives = pos_ref[...]
    mine = core * chips + chip
    total = shards * SLOT
    ids = lax.broadcasted_iota(jnp.int32, (total, rows), 0)
    ids = caps * (ids // SLOT) + ids % caps
    piece = (lax.broadcasted_iota(jnp.int32, (total, lanes), 0) % SLOT) // caps

    def dp_chip(k, i, source):
        block = dp.at[i, core, source]
        return to_chip(k, block, block, ds_sem.at[k, i], dr_sem.at[source, i])

    def dp_mate(i, source, side):
        block = dp.at[i, side, source]
        return to_mate(block, block, ms_sem.at[source, i], mr_sem.at[source, i])

    def score(i):
        each(1, chips, lambda k: part_copy(k, i, chip_peer(k), chip_peer(k)).wait_recv())
        start = pl.multiple_of(chip * rows, rows)
        projected = own[i, pl.ds(start, rows), :]
        for k in range(1, chips):
            projected = projected + xr[chip_peer(k), i].astype(F32)
        scale = lax.rsqrt(jnp.sum(projected * projected, axis=1, keepdims=True) + eps_norm)
        unit = projected * scale
        unit_half = unit.astype(BF16)
        logits = logit_scale * lax.dot_general(
            tab[...], unit_half, (((1,), (1,)), ((), ())), preferred_element_type=F32
        )
        expon = jnp.exp(logits)
        probs = expon * (packs / jnp.sum(expon, axis=0, keepdims=True))
        index = positives[:, i * both : i * both + rows]
        for j in range(1, sections):
            low = i * both + j * rows
            index = jnp.where(mine == j, positives[:, low : low + rows], index)
        onehot = (ids == index).astype(F32)
        dlogits = (probs - onehot).astype(BF16)
        dunit = (logit_scale / packs) * lax.dot_general(
            dlogits, tab[...], (((0,), (0,)), ((), ())), preferred_element_type=F32
        )
        dproj = scale * (dunit - unit * jnp.sum(unit * dunit, axis=1, keepdims=True))
        dp[i, core, chip] = dproj.astype(BF16)
        each(1, chips, lambda k: dp_chip(k, i, chip).start())
        dp_mate(i, chip, core).start()
        term = jnp.zeros((total, lanes), F32)
        for q in range(packs):
            value = jnp.dot(
                dlogits, unit_half[:, q * lanes : (q + 1) * lanes], preferred_element_type=F32
            )
            term = jnp.where(piece == q, value, term)
        dacc[...] = term if i == 0 else dacc[...] + term

    def forward(i):
        def one(k):
            dp_chip(k, i, chip_peer(k)).wait_recv()
            dp_mate(i, chip_peer(k), core).start()

        each(1, chips, one)

    def grad(i):
        each(0, chips, lambda c: dp_mate(i, c, 1 - core).wait_recv())
        og[i] = lax.dot_general(
            dp[i].reshape(both, width), wv[...], (((1,), (1,)), ((), ())),
            preferred_element_type=F32,
        ).astype(BF16)
        og_copy(i).start()

    sum_copy = to_mate(dacc, dpt, as_sem, ar_sem)

    def give_copy(k, there, here):
        return to_shard(k, dsnd.at[there], drc.at[here], gs_sem.at[k], gr_sem.at[here])

    def end_copy(k, source):
        return to_chip(k, fin.at[source], fin.at[source], es_sem.at[k], er_sem.at[source])

    for i in range(n_chunks):
        score(i)
    sum_copy.start()
    forward(0)
    sum_copy.wait_recv()
    dsnd[...] = (dacc[...] + dpt[...]).astype(BF16).reshape(shards, SLOT, lanes)
    each(1, shards, lambda k: give_copy(k, shard_peer(k), t).start())
    drc[t] = dsnd[t]
    for i in range(n_chunks):
        grad(i)
        if i < n_chunks - 1:
            forward(i + 1)
    each(1, shards, lambda k: give_copy(k, shard_peer(k), shard_peer(k)).wait_recv())
    fin[chip] = jnp.sum(drc[...].astype(F32), axis=0)
    each(1, chips, lambda k: end_copy(k, chip).start())
    each(1, chips, lambda k: end_copy(k, chip_peer(k)).wait_recv())
    dcap = logit_scale * jnp.sum(fin[...], axis=0)
    dcap = jnp.concatenate(
        [dcap[q * caps : (q + 1) * caps, :] for q in range(packs)], axis=1
    )
    cg_ref[...] = cap_scale * (
        dcap - cap_unit * jnp.sum(cap_unit * dcap, axis=1, keepdims=True)
    )

    for i in range(n_chunks):
        og_copy(i).wait()
        mate_copy(i).wait_send()
        each(1, chips, lambda k: part_copy(k, i, chip_peer(k), chip).wait_send())
        each(1, chips, lambda k: dp_chip(k, i, chip).wait_send())
        each(0, chips, lambda c: dp_mate(i, c, core).wait_send())
    sum_copy.wait_send()
    each(1, shards, lambda k: cap_copy(k, t).wait_send())
    each(1, shards, lambda k: give_copy(k, shard_peer(k), t).wait_send())
    each(1, chips, lambda k: end_copy(k, chip).wait_send())


def write_out(rg_in, cg_in, rg_out, cg_out, rg_buf, cg_buf, in_sem, out_sem):
    rows = rg_in.shape[0] // COPIES
    moves = []
    for i in range(COPIES):
        band = pl.ds(i * rows, rows)
        moves.append((rg_in.at[band, :], rg_buf.at[band, :], rg_out.at[band, :]))
    moves.append((cg_in, cg_buf, cg_out))
    loads = [pltpu.make_async_copy(a, b, in_sem.at[j]) for j, (a, b, c) in enumerate(moves)]
    stores = [pltpu.make_async_copy(b, c, out_sem.at[j]) for j, (a, b, c) in enumerate(moves)]
    for load in loads:
        load.start()
    for load, store in zip(loads, stores):
        load.wait()
        store.start()
    for store in stores:
        store.wait()


def solution(mesh):
    sections, shards = mesh.shape["section"], mesh.shape["shard"]
    chips = sections // 2

    def on_device(features, proj_weight, captions, positives):
        n_rows, depth = features.shape
        width = proj_weight.shape[1]
        caps = captions.shape[0]
        lanes = width * caps // SLOT
        n = CHUNKS
        rows = n_rows // sections // n
        half = chips * rows
        dma = pltpu.SemaphoreType.DMA
        any_space = pl.BlockSpec(memory_space=pl.ANY)
        vmem = pl.BlockSpec(memory_space=pltpu.VMEM)
        flops = 4 * n_rows * depth * width
        shapes = (
            jax.ShapeDtypeStruct((n_rows, depth), BF16),
            jax.ShapeDtypeStruct((caps, width), F32),
        )
        grads = pl.pallas_call(
            functools.partial(kernel, sections, shards),
            out_shape=shapes,
            in_specs=[any_space, any_space, vmem, vmem],
            out_specs=(any_space, vmem),
            scratch_shapes=[
                pltpu.VMEM((n, 2, half, depth), BF16),
                pltpu.VMEM((depth, width), BF16),
                pltpu.VMEM((n, half, width), F32),
                pltpu.VMEM((n, half, width), BF16),
                pltpu.VMEM((n, half, width), BF16),
                pltpu.VMEM((n, chips, rows, width), BF16),
                pltpu.VMEM((chips, n, rows, width), BF16),
                pltpu.VMEM((n, 2, chips, rows, width), BF16),
                pltpu.VMEM((n, 2 * half, depth), BF16),
                pltpu.VMEM((shards, SLOT, lanes), BF16),
                pltpu.VMEM((shards * SLOT, width), BF16),
                pltpu.VMEM((shards * SLOT, lanes), F32),
                pltpu.VMEM((shards * SLOT, lanes), F32),
                pltpu.VMEM((shards, SLOT, lanes), BF16),
                pltpu.VMEM((shards, SLOT, lanes), BF16),
                pltpu.VMEM((chips, SLOT, lanes), F32),
                dma((n, 2)), dma((PIECES,)), dma((n,)),
                dma((n,)), dma((n,)),
                dma((chips, n)), dma((chips, n)),
                dma((chips, n)), dma((chips, n)),
                dma((chips, n)), dma((chips, n)),
                dma((shards,)), dma((shards,)),
                dma, dma,
                dma((shards,)), dma((shards,)),
                dma((chips,)), dma((chips,)),
            ],
            cost_estimate=pl.CostEstimate(
                flops=flops,
                bytes_accessed=2 * (2 * n_rows * depth + depth * width),
                transcendentals=0,
            ),
            compiler_params=pltpu.CompilerParams(
                collective_id=0, has_side_effects=True, vmem_limit_bytes=56 * 1024 * 1024
            ),
        )(features, proj_weight, captions, positives.reshape(1, n_rows))
        return pl.pallas_call(
            write_out,
            out_shape=shapes,
            in_specs=[any_space, any_space],
            out_specs=(any_space, any_space),
            scratch_shapes=[
                pltpu.VMEM((n_rows, depth), BF16),
                pltpu.VMEM((caps, width), F32),
                dma((COPIES + 1,)), dma((COPIES + 1,)),
            ],
            cost_estimate=pl.CostEstimate(
                flops=0, bytes_accessed=4 * n_rows * depth, transcendentals=0
            ),
        )(*grads)

    return jax.shard_map(
        on_device,
        mesh=mesh,
        in_specs=(P("shard", "section"), P("section", None), P("shard", None), P("shard")),
        out_specs=(P("shard", "section"), P("shard", None)),
        check_vma=False,
    )
```

time: 49.7 us -> 27.4 us (0.55)
  Pallas kernels: 48.8 us -> 26.6 us
    pallas_call x1, Pallas kernels: 25.5 us -> 1.98 us  [on_device(): pl.pallas_call(write_out, out_shape=shapes, in_specs=[any_space, any_spac...]
    pallas_call x1, Pallas kernels: 23.3 us -> 24.6 us  [on_device(): pl.pallas_call(functools.partial(kernel, sections, shards), out_shape=sha...]
where the time goes in v3:
time: 27.4 us; the launch traced here: 27.2 us
  Pallas kernels  26.6 us (97%)
  between operations  0.64 us (2%)
    pallas_call x1, Pallas kernels, on_device(): pl.pallas_call(functools.partial(kernel, sections, shards), out_shape=sha...  24.6 us
    pallas_call x1, Pallas kernels, on_device(): pl.pallas_call(write_out, out_shape=shapes, in_specs=[any_space, any_spac...  1.98 us

profile of v3, /device:TPU:0, one launch (start us, length us, event | category | flops | bytes accessed | tf_op | source)
XLA Modules:
  0.0 27.2 jit_solution(17908634611892413851)
XLA Ops:
  0.6 24.6 %shard_map.59 = (bf16[256,1536]{1,0:T(8,128)(2,1)}, f32[4,1024]{1,0:T(4,128)}) custom-call(bf16[256,1536]{1,0:T(8,128)(2,1)} %f_hbm.1, bf16[1536,1024]{1,0:T(8,128)(2,1)} %w_hbm.1, bf16[4,1024]{1,0:T(4,128)(2,1)} %cap_ref.1, s32[1,256]{1,0:T(1,128)} %bitcast.1), custom_call_target="tpu_custom_call" | custom-call | flops 1610612736 | bytes 4718592 | tf_op jit(solution)/shard_map/pallas_call | solution.py:325
  25.2 2.0 %shard_map.60 = (bf16[256,1536]{1,0:T(8,128)(2,1)}, f32[4,1024]{1,0:T(4,128)}) custom-call(bf16[256,1536]{1,0:T(8,128)(2,1)} %get-tuple-element.4.rg_in, f32[4,1024]{1,0:T(4,128)} %get-tuple-element.5.cg_in), custom_call_target="tpu_custom_call" | custom-call | bytes 1572864 | tf_op jit(solution)/shard_map/pallas_call | solution.py:366

commit v4 on v3

--- a/solution.py
+++ b/solution.py
@@ -27,9 +27,9 @@
 
 
 def kernel(
-    sections, shards, f_hbm, w_hbm, cap_ref, pos_ref, rg_hbm, cg_ref,
-    fv, wv, own, psnd, prcv, xs, xr, dp, og, cs, tab, dacc, dpt, dsnd, drc, fin,
-    f_sem, w_sem, og_sem, ps_sem, pr_sem, xs_sem, xr_sem, ms_sem, mr_sem, ds_sem, dr_sem,
+    sections, shards, f_hbm, w_hbm, cap_ref, pos_ref, rg_ref, cg_ref,
+    fv, wv, own, psnd, prcv, xs, xr, dp, cs, tab, dacc, dpt, dsnd, drc, fin,
+    f_sem, w_sem, ps_sem, pr_sem, xs_sem, xr_sem, ms_sem, mr_sem, ds_sem, dr_sem,
     cs_sem, cr_sem, as_sem, ar_sem, gs_sem, gr_sem, es_sem, er_sem,
 ):
     chips = sections // 2
@@ -86,11 +86,6 @@
         band = pl.ds(p * step, step)
         return pltpu.make_async_copy(w_hbm.at[band, :], wv.at[band, :], w_sem.at[p])
 
-    def og_copy(i):
-        return pltpu.make_async_copy(
-            og.at[i], rg_hbm.at[pl.ds(i * both, both), :], og_sem.at[i]
-        )
-
     for which in range(2):
         f_copy(0, which).start()
     for p in range(PIECES):
@@ -135,18 +130,17 @@
     for i in range(n_chunks):
         for which in range(2):
             f_copy(i, which).wait()
-        if i == 0:
-            part = None
-            for p in range(PIECES):
+        part = None
+        for p in range(PIECES):
+            if i == 0:
                 w_copy(p).wait()
-                band = slice(p * step, (p + 1) * step)
-                term = jnp.dot(
-                    fv[i, :, :, band].reshape(both, step), wv[band, :],
-                    preferred_element_type=F32,
-                )
-                part = term if part is None else part + term
-        else:
-            part = jnp.dot(fv[i].reshape(both, depth), wv[...], preferred_element_type=F32)
+            band = slice(p * step, (p + 1) * step)
+            term = jnp.dot(
+                fv[i, :, :, band].reshape(both, step), wv[band, :], preferred_element_type=F32
+            )
+            part = term if part is None else part + term
+            if i >= 1 and p == PIECES - 2:
+                chip_sum(i - 1)
         psnd[i] = part[:half].astype(BF16)
         own[i] = part[half:]
         if i == 0:
@@ -154,8 +148,6 @@
         mate_copy(i).start()
         if i == 0:
             each(1, shards, lambda k: cap_copy(k, t).start())
-        if i >= 1:
-            chip_sum(i - 1)
     chip_sum(n_chunks - 1)
 
     each(1, shards, lambda k: cap_copy(k, shard_peer(k)).wait_recv())
@@ -232,13 +224,15 @@
 
         each(1, chips, one)
 
-    def grad(i):
-        each(0, chips, lambda c: dp_mate(i, c, 1 - core).wait_recv())
-        og[i] = lax.dot_general(
-            dp[i].reshape(both, width), wv[...], (((1,), (1,)), ((), ())),
+    def grad(i, part, parts):
+        if part == 0:
+            each(0, chips, lambda c: dp_mate(i, c, 1 - core).wait_recv())
+        size = depth // parts
+        band = slice(part * size, (part + 1) * size)
+        rg_ref[i * both : (i + 1) * both, band] = lax.dot_general(
+            dp[i].reshape(both, width), wv[band, :], (((1,), (1,)), ((), ())),
             preferred_element_type=F32,
         ).astype(BF16)
-        og_copy(i).start()
 
     sum_copy = to_mate(dacc, dpt, as_sem, ar_sem)
 
@@ -256,13 +250,14 @@
     dsnd[...] = (dacc[...] + dpt[...]).astype(BF16).reshape(shards, SLOT, lanes)
     each(1, shards, lambda k: give_copy(k, shard_peer(k), t).start())
     drc[t] = dsnd[t]
-    for i in range(n_chunks):
-        grad(i)
-        if i < n_chunks - 1:
-            forward(i + 1)
+    for i in range(n_chunks - 1):
+        grad(i, 0, 1)
+        forward(i + 1)
+    grad(n_chunks - 1, 0, 2)
     each(1, shards, lambda k: give_copy(k, shard_peer(k), shard_peer(k)).wait_recv())
     fin[chip] = jnp.sum(drc[...].astype(F32), axis=0)
     each(1, chips, lambda k: end_copy(k, chip).start())
+    grad(n_chunks - 1, 1, 2)
     each(1, chips, lambda k: end_copy(k, chip_peer(k)).wait_recv())
     dcap = logit_scale * jnp.sum(fin[...], axis=0)
     dcap = jnp.concatenate(
@@ -273,7 +268,6 @@
     )
 
     for i in range(n_chunks):
-        og_copy(i).wait()
         mate_copy(i).wait_send()
         each(1, chips, lambda k: part_copy(k, i, chip_peer(k), chip).wait_send())
         each(1, chips, lambda k: dp_chip(k, i, chip).wait_send())
@@ -284,22 +278,16 @@
     each(1, chips, lambda k: end_copy(k, chip).wait_send())
 
 
-def write_out(rg_in, cg_in, rg_out, cg_out, rg_buf, cg_buf, in_sem, out_sem):
+def write_out(rg_in, cg_in, rg_out, cg_out, sem):
     rows = rg_in.shape[0] // COPIES
-    moves = []
+    copies = [pltpu.make_async_copy(cg_in, cg_out, sem.at[COPIES])]
     for i in range(COPIES):
         band = pl.ds(i * rows, rows)
-        moves.append((rg_in.at[band, :], rg_buf.at[band, :], rg_out.at[band, :]))
-    moves.append((cg_in, cg_buf, cg_out))
-    loads = [pltpu.make_async_copy(a, b, in_sem.at[j]) for j, (a, b, c) in enumerate(moves)]
-    stores = [pltpu.make_async_copy(b, c, out_sem.at[j]) for j, (a, b, c) in enumerate(moves)]
-    for load in loads:
-        load.start()
-    for load, store in zip(loads, stores):
-        load.wait()
-        store.start()
-    for store in stores:
-        store.wait()
+        copies.append(pltpu.make_async_copy(rg_in.at[band, :], rg_out.at[band, :], sem.at[i]))
+    for copy in copies:
+        copy.start()
+    for copy in copies:
+        copy.wait()
 
 
 def solution(mesh):
@@ -324,9 +312,11 @@
         )
         grads = pl.pallas_call(
             functools.partial(kernel, sections, shards),
-            out_shape=shapes,
+            out_shape=(
+                pltpu.VMEM((n_rows, depth), BF16), pltpu.VMEM((caps, width), F32)
+            ),
             in_specs=[any_space, any_space, vmem, vmem],
-            out_specs=(any_space, vmem),
+            out_specs=(vmem, vmem),
             scratch_shapes=[
                 pltpu.VMEM((n, 2, half, depth), BF16),
                 pltpu.VMEM((depth, width), BF16),
@@ -336,7 +326,6 @@
                 pltpu.VMEM((n, chips, rows, width), BF16),
                 pltpu.VMEM((chips, n, rows, width), BF16),
                 pltpu.VMEM((n, 2, chips, rows, width), BF16),
-                pltpu.VMEM((n, 2 * half, depth), BF16),
                 pltpu.VMEM((shards, SLOT, lanes), BF16),
                 pltpu.VMEM((shards * SLOT, width), BF16),
                 pltpu.VMEM((shards * SLOT, lanes), F32),
@@ -344,7 +333,7 @@
                 pltpu.VMEM((shards, SLOT, lanes), BF16),
                 pltpu.VMEM((shards, SLOT, lanes), BF16),
                 pltpu.VMEM((chips, SLOT, lanes), F32),
-                dma((n, 2)), dma((PIECES,)), dma((n,)),
+                dma((n, 2)), dma((PIECES,)),
                 dma((n,)), dma((n,)),
                 dma((chips, n)), dma((chips, n)),
                 dma((chips, n)), dma((chips, n)),
@@ -366,12 +355,10 @@
         return pl.pallas_call(
             write_out,
             out_shape=shapes,
-            in_specs=[any_space, any_space],
+            in_specs=[vmem, vmem],
             out_specs=(any_space, any_space),
             scratch_shapes=[
-                pltpu.VMEM((n_rows, depth), BF16),
-                pltpu.VMEM((caps, width), F32),
-                dma((COPIES + 1,)), dma((COPIES + 1,)),
+                dma((COPIES + 1,)),
             ],
             cost_estimate=pl.CostEstimate(
                 flops=0, bytes_accessed=4 * n_rows * depth, transcendentals=0

time: 27.4 us -> 28.3 us (1.033)
  local copies, waits for them, and re-layouts: 0 us -> 1.48 us
  Pallas kernels: 26.6 us -> 26 us
    unnamed x0 -> x4, local copies, waits for them, and re-layouts: none -> 1.48 us
    pallas_call x2, Pallas kernels: 26.6 us -> 26 us  [the longest x1 24 us: on_device(): pl.pallas_call(functools.partial(kernel, sections, shards), out_shape=(pl...]
where the time goes in v4:
time: 28.3 us; the launch traced here: 28.1 us
  Pallas kernels  26 us (92%)
  local copies, waits for them, and re-layouts  1.48 us (5%)
  between operations  0.65 us (2%)
    pallas_call x1, Pallas kernels, on_device(): pl.pallas_call(functools.partial(kernel, sections, shards), out_shape=(pl...  24 us
    pallas_call x1, Pallas kernels, on_device(): pl.pallas_call(write_out, out_shape=shapes, in_specs=[vmem, vmem], out_sp...  2.05 us
    unnamed x4, local copies, waits for them, and re-layouts  1.48 us

profile of v4, /device:TPU:0, one launch (start us, length us, event | category | flops | bytes accessed | tf_op | source)
XLA Modules:
  0.0 28.1 jit_solution(7120161187614902101)
XLA Ops:
  0.6 24.0 %shard_map.59 = (bf16[256,1536]{1,0:T(8,128)(2,1)S(1)}, f32[4,1024]{1,0:T(4,128)S(1)}) custom-call(bf16[256,1536]{1,0:T(8,128)(2,1)} %f_hbm.1, bf16[1536,1024]{1,0:T(8,128)(2,1)} %w_hbm.1, bf16[4,1024]{1,0:T(4,128)(2,1)} %cap_ref.1, s32[1,256]{1,0:T(1,128)} %bitcast.1), custom_call_target="tpu_custom_call" | custom-call | flops 1610612736 | bytes 4718592 | tf_op jit(solution)/shard_map/pallas_call | solution.py:313
  24.6 0.0 copy-start
  24.6 0.9 %copy-done = bf16[256,1536]{1,0:T(8,128)(2,1)} copy-done((bf16[256,1536]{1,0:T(8,128)(2,1)}, bf16[256,1536]{1,0:T(8,128)(2,1)S(1)}, u32[]{:S(2)}) %copy-start) | copy-done | bytes 786456
  25.5 0.0 copy-start.1
  25.5 0.6 %copy-done.1 = f32[4,1024]{1,0:T(4,128)} copy-done((f32[4,1024]{1,0:T(4,128)}, f32[4,1024]{1,0:T(4,128)S(1)}, u32[]{:S(2)}) %copy-start.1) | copy-done | bytes 16408
  26.1 2.1 %shard_map.60 = (bf16[256,1536]{1,0:T(8,128)(2,1)}, f32[4,1024]{1,0:T(4,128)}) custom-call(bf16[256,1536]{1,0:T(8,128)(2,1)} %copy-done, f32[4,1024]{1,0:T(4,128)} %copy-done.1), custom_call_target="tpu_custom_call" | custom-call | bytes 1572864 | tf_op jit(solution)/shard_map/pallas_call | solution.py:355
Async XLA Ops:
  24.6 0.9 %copy-start = (bf16[256,1536]{1,0:T(8,128)(2,1)}, bf16[256,1536]{1,0:T(8,128)(2,1)S(1)}, u32[]{:S(2)}) copy-start(bf16[256,1536]{1,0:T(8,128)(2,1)S(1)} %get-tuple-element.4.rg_in) | copy-start | bytes 2359300
  25.5 0.6 %copy-start.1 = (f32[4,1024]{1,0:T(4,128)}, f32[4,1024]{1,0:T(4,128)S(1)}, u32[]{:S(2)}) copy-start(f32[4,1024]{1,0:T(4,128)S(1)} %get-tuple-element.5.cg_in) | copy-start | bytes 49156

commit v5 on v4

--- a/solution.py
+++ b/solution.py
@@ -14,7 +14,6 @@
 BF16 = jnp.bfloat16
 SLOT = 16
 CHUNKS = 2
-COPIES = 4
 PIECES = 3
 
 
@@ -278,18 +277,6 @@
     each(1, chips, lambda k: end_copy(k, chip).wait_send())
 
 
-def write_out(rg_in, cg_in, rg_out, cg_out, sem):
-    rows = rg_in.shape[0] // COPIES
-    copies = [pltpu.make_async_copy(cg_in, cg_out, sem.at[COPIES])]
-    for i in range(COPIES):
-        band = pl.ds(i * rows, rows)
-        copies.append(pltpu.make_async_copy(rg_in.at[band, :], rg_out.at[band, :], sem.at[i]))
-    for copy in copies:
-        copy.start()
-    for copy in copies:
-        copy.wait()
-
-
 def solution(mesh):
     sections, shards = mesh.shape["section"], mesh.shape["shard"]
     chips = sections // 2
@@ -306,11 +293,7 @@
         any_space = pl.BlockSpec(memory_space=pl.ANY)
         vmem = pl.BlockSpec(memory_space=pltpu.VMEM)
         flops = 4 * n_rows * depth * width
-        shapes = (
-            jax.ShapeDtypeStruct((n_rows, depth), BF16),
-            jax.ShapeDtypeStruct((caps, width), F32),
-        )
-        grads = pl.pallas_call(
+        return pl.pallas_call(
             functools.partial(kernel, sections, shards),
             out_shape=(
                 pltpu.VMEM((n_rows, depth), BF16), pltpu.VMEM((caps, width), F32)
@@ -352,19 +335,6 @@
                 collective_id=0, has_side_effects=True, vmem_limit_bytes=56 * 1024 * 1024
             ),
         )(features, proj_weight, captions, positives.reshape(1, n_rows))
-        return pl.pallas_call(
-            write_out,
-            out_shape=shapes,
-            in_specs=[vmem, vmem],
-            out_specs=(any_space, any_space),
-            scratch_shapes=[
-                dma((COPIES + 1,)),
-            ],
-            cost_estimate=pl.CostEstimate(
-                flops=0, bytes_accessed=4 * n_rows * depth, transcendentals=0
-            ),
-        )(*grads)
-
     return jax.shard_map(
         on_device,
         mesh=mesh,

time: 28.3 us -> 26.3 us (0.929)
  Pallas kernels: 26 us -> 24 us
    pallas_call x1 -> x0, Pallas kernels: 2.05 us -> none  [on_device(): pl.pallas_call(write_out, out_shape=shapes, in_specs=[vmem, vmem], out_sp...]
    unnamed x4 -> x2, local copies, waits for them, and re-layouts: 1.48 us -> 1.49 us
where the time goes in v5:
time: 26.3 us; the launch traced here: 26.1 us
  Pallas kernels  24 us (91%)
  local copies, waits for them, and re-layouts  1.49 us (6%)
  between operations  0.64 us (2%)
    pallas_call x1, Pallas kernels, on_device(): pl.pallas_call(functools.partial(kernel, sections, shards), out_shape=(pl...  24 us
    unnamed x2, local copies, waits for them, and re-layouts  1.49 us

profile of v5, /device:TPU:0, one launch (start us, length us, event | category | flops | bytes accessed | tf_op | source)
XLA Modules:
  0.0 26.1 jit_solution(15928567860343192243)
XLA Ops:
  0.6 24.0 %shard_map.59 = (bf16[256,1536]{1,0:T(8,128)(2,1)S(1)}, f32[4,1024]{1,0:T(4,128)S(1)}) custom-call(bf16[256,1536]{1,0:T(8,128)(2,1)} %f_hbm.1, bf16[1536,1024]{1,0:T(8,128)(2,1)} %w_hbm.1, bf16[4,1024]{1,0:T(4,128)(2,1)} %cap_ref.1, s32[1,256]{1,0:T(1,128)} %bitcast.1), custom_call_target="tpu_custom_call" | custom-call | flops 1610612736 | bytes 4718592 | tf_op jit(solution)/shard_map/pallas_call | solution.py:296
  24.6 0.9 %copy.8 = bf16[256,1536]{1,0:T(8,128)(2,1)} copy(bf16[256,1536]{1,0:T(8,128)(2,1)S(1)} %get-tuple-element.2) | data formatting | bytes 1572864
  25.5 0.6 %copy.9 = f32[4,1024]{1,0:T(4,128)} copy(f32[4,1024]{1,0:T(4,128)S(1)} %get-tuple-element.3) | data formatting | bytes 32768

commit v6 on v5

--- a/solution.py
+++ b/solution.py
@@ -181,6 +181,8 @@
         block = dp.at[i, side, source]
         return to_mate(block, block, ms_sem.at[source, i], mr_sem.at[source, i])
 
+    sum_copy = to_mate(dacc, dpt, as_sem, ar_sem)
+
     def score(i):
         each(1, chips, lambda k: part_copy(k, i, chip_peer(k), chip_peer(k)).wait_recv())
         start = pl.multiple_of(chip * rows, rows)
@@ -201,13 +203,6 @@
             index = jnp.where(mine == j, positives[:, low : low + rows], index)
         onehot = (ids == index).astype(F32)
         dlogits = (probs - onehot).astype(BF16)
-        dunit = (logit_scale / packs) * lax.dot_general(
-            dlogits, tab[...], (((0,), (0,)), ((), ())), preferred_element_type=F32
-        )
-        dproj = scale * (dunit - unit * jnp.sum(unit * dunit, axis=1, keepdims=True))
-        dp[i, core, chip] = dproj.astype(BF16)
-        each(1, chips, lambda k: dp_chip(k, i, chip).start())
-        dp_mate(i, chip, core).start()
         term = jnp.zeros((total, lanes), F32)
         for q in range(packs):
             value = jnp.dot(
@@ -215,6 +210,15 @@
             )
             term = jnp.where(piece == q, value, term)
         dacc[...] = term if i == 0 else dacc[...] + term
+        if i == n_chunks - 1:
+            sum_copy.start()
+        dunit = (logit_scale / packs) * lax.dot_general(
+            dlogits, tab[...], (((0,), (0,)), ((), ())), preferred_element_type=F32
+        )
+        dproj = scale * (dunit - unit * jnp.sum(unit * dunit, axis=1, keepdims=True))
+        dp[i, core, chip] = dproj.astype(BF16)
+        each(1, chips, lambda k: dp_chip(k, i, chip).start())
+        dp_mate(i, chip, core).start()
 
     def forward(i):
         def one(k):
@@ -233,8 +237,6 @@
             preferred_element_type=F32,
         ).astype(BF16)
 
-    sum_copy = to_mate(dacc, dpt, as_sem, ar_sem)
-
     def give_copy(k, there, here):
         return to_shard(k, dsnd.at[there], drc.at[here], gs_sem.at[k], gr_sem.at[here])
 
@@ -243,7 +245,6 @@
 
     for i in range(n_chunks):
         score(i)
-    sum_copy.start()
     forward(0)
     sum_copy.wait_recv()
     dsnd[...] = (dacc[...] + dpt[...]).astype(BF16).reshape(shards, SLOT, lanes)

time: 26.3 us -> 26.3 us (level)
  no operation moved by 1% of the time
where the time goes in v6:
time: 26.3 us; the launch traced here: 26.1 us
  Pallas kernels  24 us (91%)
  local copies, waits for them, and re-layouts  1.49 us (6%)
  between operations  0.64 us (2%)
    pallas_call x1, Pallas kernels, on_device(): pl.pallas_call(functools.partial(kernel, sections, shards), out_shape=(pl...  24 us
    unnamed x2, local copies, waits for them, and re-layouts  1.49 us

profile of v6, /device:TPU:0, one launch (start us, length us, event | category | flops | bytes accessed | tf_op | source)
XLA Modules:
  0.0 26.1 jit_solution(1986705506274918710)
XLA Ops:
  0.6 24.0 %shard_map.59 = (bf16[256,1536]{1,0:T(8,128)(2,1)S(1)}, f32[4,1024]{1,0:T(4,128)S(1)}) custom-call(bf16[256,1536]{1,0:T(8,128)(2,1)} %f_hbm.1, bf16[1536,1024]{1,0:T(8,128)(2,1)} %w_hbm.1, bf16[4,1024]{1,0:T(4,128)(2,1)} %cap_ref.1, s32[1,256]{1,0:T(1,128)} %bitcast.1), custom_call_target="tpu_custom_call" | custom-call | flops 1610612736 | bytes 4718592 | tf_op jit(solution)/shard_map/pallas_call | solution.py:297
  24.6 0.9 %copy.8 = bf16[256,1536]{1,0:T(8,128)(2,1)} copy(bf16[256,1536]{1,0:T(8,128)(2,1)S(1)} %get-tuple-element.2) | data formatting | bytes 1572864
  25.5 0.6 %copy.9 = f32[4,1024]{1,0:T(4,128)} copy(f32[4,1024]{1,0:T(4,128)S(1)} %get-tuple-element.3) | data formatting | bytes 32768
